TPU v7x, 512 devices: a whole 4x4x16 slice. The times are simulated.
512 devices in a mesh: agent: 16 (over x, y), dp: 32 (over z, core).
Axes of the slice: x: 4, y: 4, z: 16, core: 2. Of those that a mesh axis runs over, the one named last changes fastest.
Arguments:
- learn_obs: bfloat16 [16, 1024, 16, 3456], P('agent', 'dp'), may hold values from -6 to 6
- own_obs: bfloat16 [16, 1024, 3456], P('agent', 'dp'), may hold values from -6 to 6
- opp_obs: bfloat16 [16, 1024, 3456], P('agent', 'dp'), may hold values from -6 to 6
- opponent: int32 [16, 1024, 1], P('agent', 'dp'), may hold values from 0 to 15; in each aligned block of 32 rows (0 to 31, 32 to 63, ..., all dimensions but the last counted through in order) at most 8 rows name the same one
- actions: int32 [16, 1024, 16], P('agent', 'dp'), may hold values from 0 to 17
- done: int32 [16, 1024, 16], P('agent', 'dp'), may hold values 0 or 1
- rewards: float32 [16, 1024, 16], P('agent', 'dp'), may hold values from -6 to 6
- behaviour: float32 [16, 1024, 16], P('agent', 'dp'), may hold values from -4.5 to -1.5
- core_master: float32 [16, 256, 3712], P('agent', 'dp'), may hold values from -0.109375 to 0.109375
- core_mom: float32 [16, 256, 3712], P('agent', 'dp'), may hold values from -6 to 6
- core_vel: float32 [16, 256, 3712], P('agent', 'dp'), may hold values from 0.1 to 1
- head_master: float32 [16, 19, 256], P('agent'), may hold values from -0.375 to 0.375
- head_mom: float32 [16, 19, 256], P('agent'), may hold values from -6 to 6
- head_vel: float32 [16, 19, 256], P('agent'), may hold values from 0.1 to 1
- rates: float32 [16], P('agent'), may hold values from 0.01 to 0.1
Outputs:
- own_logits: float32 [16, 1024, 18], P('agent', 'dp')
- opp_logits: bfloat16 [16, 1024, 18], P('agent', 'dp')
- new_core: float32 [16, 256, 3712], P('agent', 'dp')
- new_core_mom: float32 [16, 256, 3712], P('agent', 'dp')
- new_core_vel: float32 [16, 256, 3712], P('agent', 'dp')
- new_head: float32 [16, 19, 256], P('agent')
- new_head_mom: float32 [16, 19, 256], P('agent')
- new_head_vel: float32 [16, 19, 256], P('agent')
Inputs may be any that keep to these rules, and one draw needn't show every extreme that they name: Among the 32 environments of one device (aligned blocks of the environment dimension), at most 8 face the same opponent agent, and some device reaches 8 in every draw.
All inputs are finite; a program needn't handle non-finite values. No bound on the sum of `done` on one device may be relied on, other than what follows from the above.
Results may differ from a plain program's by a relative error of at most 0.023.
Values may be sent and summed in bfloat16 or wider, within the bound.
A program may use at most 64 MiB of HBM per device.

v0:
```python
import jax
import jax.numpy as jnp
from jax import lax
from jax.sharding import Mesh
from jax.sharding import PartitionSpec as P

BLOCK = 128
DP = ("dp_0", "dp_1")
gamma_rate = 0.99
baseline_cost = 0.5
entropy_cost = 0.05
beta_first = 0.9
beta_second = 0.99
adam_eps = 1e-08


def joined_along(blocks, dim):
    shape = list(blocks.shape[1:])
    shape[dim] *= blocks.shape[0]
    return jnp.moveaxis(blocks, 0, dim).reshape(shape)


def stacked_from(x, axes, order):
    blocks = x[None]
    for k in order:
        blocks = lax.all_gather(blocks, axes[k], axis=0, tiled=True)
    current = [lax.axis_size(axes[k]) for k in reversed(order)]
    blocks = blocks.reshape(*current, *x.shape)
    turned = sorted(range(len(order)), key=lambda place: order[len(order) - 1 - place])
    return blocks.transpose(*turned, *range(len(order), blocks.ndim)).reshape(-1, *x.shape)


def gather_axes(x, axes, order, dim):
    return joined_along(stacked_from(x, axes, order), dim)


def reduced_to_own(blocks, axes, order):
    shape = [lax.axis_size(a) for a in axes]
    blocks = blocks.reshape(*shape, *blocks.shape[1:])
    blocks = blocks.transpose(*order, *range(len(axes), blocks.ndim))
    blocks = blocks.reshape(-1, *blocks.shape[len(axes) :])
    for k in order:
        blocks = lax.psum_scatter(blocks, axes[k], scatter_dimension=0, tiled=True)
    return blocks[0]


def in_blocks(x, dim, peers):
    before, after = (x.shape[:dim], x.shape[dim + 1 :])
    return jnp.moveaxis(x.reshape(*before, peers, -1, *after), dim, 0)


def sum_by_axis(x, axes, order, dim):
    peers = lax.axis_size(axes)
    return reduced_to_own(in_blocks(x, dim, peers), axes, order)


def by_axis(x, axes):
    for axis in axes:
        x = lax.psum(x, axis)
    return x


def contract(left, right):
    return lax.dot_general(
        left, right, (((1,), (1,)), ((), ())), preferred_element_type=jnp.float32
    )


def contract_rows(left, right):
    return lax.dot_general(
        left, right, (((0,), (0,)), ((), ())), preferred_element_type=jnp.float32
    )


def forward(inputs, core_bf, head_bf):
    width = inputs.shape[-1]
    pre_one = contract(inputs, core_bf[:, :width])
    first_act = jax.nn.relu(pre_one)
    first_bf = first_act.astype(jnp.bfloat16)
    pre_two = contract(first_bf, core_bf[:, width:])
    second_act = jax.nn.relu(pre_two) + first_act
    second_bf = second_act.astype(jnp.bfloat16)
    network_outputs = contract(second_bf, head_bf)
    return (network_outputs, pre_one, first_bf, pre_two, second_bf)


def importance_trace_gradients(
    network_outputs, bootstrap_value, actions, done, rewards, behaviour, scale_factor
):
    action_count = network_outputs.shape[-1] - 1
    logits = network_outputs[..., :action_count]
    values = network_outputs[..., action_count]
    totals = jnp.sum(jnp.exp(logits), -1)
    logp = logits - jnp.log(totals)[..., None]
    probs = jnp.exp(logp)
    chosen = (actions[..., None] == jnp.arange(action_count, dtype=jnp.int32)).astype(jnp.float32)
    logp_act = jnp.sum(logp * chosen, -1)
    ratio = jnp.minimum(1.0, jnp.exp(logp_act - behaviour))
    discount = gamma_rate * (1.0 - done.astype(jnp.float32))
    next_values = jnp.concatenate([values[:, 1:], bootstrap_value[:, None]], 1)
    deltas = ratio * (rewards + discount * next_values - values)

    def backstep(carry, item):
        delta, factor = item
        carry = delta + factor * carry
        return (carry, carry)

    start = jnp.zeros((values.shape[0],), jnp.float32)
    final_carry, corrections = lax.scan(
        backstep, start, (deltas.T, (discount * ratio).T), reverse=True
    )
    targets = values + corrections.T
    next_targets = jnp.concatenate([targets[:, 1:], bootstrap_value[:, None]], 1)
    advantage = ratio * (rewards + discount * next_targets - values)
    entropy = -jnp.sum(probs * logp, -1)
    grad_logits = scale_factor * (
        -advantage[..., None] * (chosen - probs)
        + entropy_cost * probs * (logp + entropy[..., None])
    )
    grad_value = scale_factor * (-baseline_cost * (targets - values))
    return jnp.concatenate([grad_logits, grad_value[..., None]], -1)


def adam_step(master, moment, second, grad, rate):
    moment = beta_first * moment + (1.0 - beta_first) * grad
    second = beta_second * second + (1.0 - beta_second) * grad * grad
    master = master - rate * moment / (jnp.sqrt(second) + adam_eps)
    return (master, moment, second)


def per_device(
    learn_obs,
    own_obs,
    opp_obs,
    opponent,
    actions,
    done,
    rewards,
    behaviour,
    core_master,
    core_mom,
    core_vel,
    head_master,
    head_mom,
    head_vel,
    rates,
):
    environment_total, rollout_length, width = (
        learn_obs.shape[1],
        learn_obs.shape[2],
        learn_obs.shape[3],
    )
    action_count = head_master.shape[1] - 1
    agent_count = lax.axis_size("agent")
    slots = min(environment_total, BLOCK // agent_count)
    scale_factor = 1.0 / rollout_length
    core_bf = gather_axes(core_master.astype(jnp.bfloat16), DP, (0, 1), 1)[0]
    head_bf = head_master[0].astype(jnp.bfloat16)
    own_out = forward(own_obs[0], core_bf, head_bf)[0]
    ids = opponent[0, :, 0]
    earlier = (ids[None, :] == ids[:, None]) & jnp.tril(jnp.ones((ids.shape[0],) * 2, bool), -1)
    ranks = jnp.sum(earlier.astype(jnp.int32), 1)
    position = ids * slots + ranks
    placing = (
        position[None, :] == jnp.arange(agent_count * slots, dtype=jnp.int32)[:, None]
    ).astype(jnp.bfloat16)
    outgoing = jnp.dot(placing, opp_obs[0], preferred_element_type=jnp.float32).astype(jnp.bfloat16)
    outgoing = outgoing.reshape(agent_count, slots, width)
    incoming = lax.all_to_all(outgoing, "agent", split_axis=0, concat_axis=0, tiled=True)
    count = incoming.shape[1]
    played = forward(incoming.reshape(agent_count * count, width), core_bf, head_bf)[0][
        :, :action_count
    ]
    played = played.astype(jnp.bfloat16).reshape(agent_count, count, action_count)
    returned = lax.all_to_all(played, "agent", split_axis=0, concat_axis=0, tiled=True)
    opp_logits = returned.reshape(agent_count * slots, action_count)[position]
    rows = learn_obs[0].reshape(environment_total * rollout_length, width)
    network_outputs, pre_one, first_bf, pre_two, second_bf = forward(rows, core_bf, head_bf)
    output_gradient = importance_trace_gradients(
        network_outputs.reshape(environment_total, rollout_length, action_count + 1),
        own_out[:, action_count],
        actions[0],
        done[0],
        rewards[0],
        behaviour[0],
        scale_factor,
    )
    grad_bf = output_gradient.reshape(environment_total * rollout_length, action_count + 1).astype(
        jnp.bfloat16
    )
    head_grad = contract_rows(grad_bf, second_bf)
    grad_second = jnp.dot(grad_bf, head_bf, preferred_element_type=jnp.float32)
    grad_pre_two = jnp.where(pre_two > 0, grad_second, 0.0).astype(jnp.bfloat16)
    grad_first = grad_second + jnp.dot(
        grad_pre_two, core_bf[:, width:], preferred_element_type=jnp.float32
    )
    grad_pre_one = jnp.where(pre_one > 0, grad_first, 0.0).astype(jnp.bfloat16)
    core_grad = sum_by_axis(
        jnp.concatenate(
            [contract_rows(grad_pre_one, rows), contract_rows(grad_pre_two, first_bf)], 1
        ).astype(jnp.bfloat16),
        DP,
        (1, 0),
        0,
    ).astype(jnp.float32)
    head_total = by_axis(head_grad, DP)
    rate = rates[0]
    new_core, new_core_mom, new_core_vel = adam_step(
        core_master[0], core_mom[0], core_vel[0], core_grad, rate
    )
    new_head, new_head_mom, new_head_vel = adam_step(
        head_master[0], head_mom[0], head_vel[0], head_total, rate
    )
    return (
        own_out[:, :action_count][None],
        opp_logits[None],
        new_core[None],
        new_core_mom[None],
        new_core_vel[None],
        new_head[None],
        new_head_mom[None],
        new_head_vel[None],
    )


def solution(mesh):
    torus = Mesh(mesh.devices.reshape(mesh.shape["agent"], 16, 2), ("agent", "dp_0", "dp_1"))
    return jax.shard_map(
        per_device,
        mesh=torus,
        in_specs=(
            P("agent", DP, None, None),
            P("agent", DP, None),
            P("agent", DP, None),
            P("agent", DP, None),
            P("agent", DP, None),
            P("agent", DP, None),
            P("agent", DP, None),
            P("agent", DP, None),
            P("agent", DP, None),
            P("agent", DP, None),
            P("agent", DP, None),
            P("agent", None, None),
            P("agent", None, None),
            P("agent", None, None),
            P("agent"),
        ),
        out_specs=(
            P("agent", DP, None),
            P("agent", DP, None),
            P("agent", DP, None),
            P("agent", DP, None),
            P("agent", DP, None),
            P("agent", None, None),
            P("agent", None, None),
            P("agent", None, None),
        ),
        check_vma=False,
    )
```

profile of v0, /device:TPU:1, one launch (start us, length us, event | category | flops | bytes accessed | tf_op | source)
XLA Modules:
  0.0 268.0 jit_solution(14837776084978435782)
XLA Ops:
  8.3 37.6 %all-gather = bf16[16,8,3712]{2,1,0:T(8,128)(2,1)} all-gather(bf16[1,8,3712]{2,1,0:T(8,128)(2,1)S(1)} %convert_element_type.71), channel_id=2, replica_groups=mesh['agent'=16,'dp_0'=16,'dp_1'=2] {'dp_0'}, dimensions={0}, use_global_device_ids=true | all-gather | bytes 1009664 | tf_op jit(solution)/shard_map/all_gather | solution.py:26
  46.8 1.4 convert_element_type.81
  48.1 22.9 %all-gather.4.cloned.1.call-done = bf16[32,8,3712]{2,1,0:T(8,128)(2,1)} async-done(((bf16[16,8,3712]{2,1,0:T(8,128)(2,1)}), bf16[32,8,3712]{2,1,0:T(8,128)(2,1)}) %all-gather.4.cloned.1.call-update) | async-done | bytes 1900560 | tf_op jit(solution)/shard_map/all_gather | solution.py:26
  71.0 1.7 copy.180
  75.3 1.8 fusion.26
  77.1 2.6 fusion.4
  80.5 2.0 add_convert_fusion
  84.2 2.3 fusion.33
  89.7 1.3 fusion.71
  91.6 40.4 %while.17 = (s32[]{:T(128)}, f32[32]{0:T(128)}, f32[16,32]{1,0:T(8,128)}, f32[16,32]{1,0:T(8,128)}, f32[16,32]{1,0:T(8,128)}, /*index=5*/s32[]{:T(128)}, s32[]{:T(128)}, s32[]{:T(128)}) while((s32[]{:T(128)}, f32[32]{0:T(128)}, f32[16,32]{1,0:T(8,128)}, f32[16,32]{1,0:T(8,128)}, f32[16,32]{1,0:T(8,128)}, /*index=5*/s32[]{:T(128)}, ...), condition=%wide.region_4.5_spmd.clone, body=%wide.region_3.4_spmd.clone.sunk | while | flops 100 | bytes 891 | solution.py:109
  133.4 1.4 copy.188
  134.7 1.4 concatenate.38
  138.1 1.3 fusion.70
  140.2 1.9 fusion.31
  142.1 1.6 copy.189
  144.8 2.1 convolution_convert_fusion.2
  147.0 1.9 fusion.14
  148.9 1.8 copy.193
  150.7 2.1 convolution_convert_fusion
  152.9 1.4 copy.194
  155.2 2.2 fusion.3
  157.4 5.6 %all-to-all-start = ((bf16[16,8,3456]{2,1,0:T(8,128)(2,1)}), bf16[16,8,3456]{2,1,0:T(8,128)(2,1)}, u32[]{:S(2)}, u32[]{:S(2)}) async-start(bf16[16,8,3456]{2,1,0:T(8,128)(2,1)} %fusion.3), calls=%async_computation | async-start | bytes 1769472 | tf_op jit(solution)/shard_map/all_to_all | solution.py:169
  163.0 12.6 %reduce-scatter.5.cloned.1.call-done = bf16[16,8,3712]{2,1,0:T(8,128)(2,1)} async-done(((bf16[32,8,3712]{2,1,0:T(8,128)(2,1)}), bf16[16,8,3712]{2,1,0:T(8,128)(2,1)}) %reduce-scatter.5.cloned.1.call-update) | async-done | bytes 950288 | tf_op jit(solution)/shard_map/reduce_scatter | solution.py:43
  176.9 3.1 %fusion.15 = f32[128,256]{1,0:T(8,128)} fusion(bf16[256,3712]{1,0:T(8,128)(2,1)} %bitcast.156, bf16[16,8,3456]{2,1,0:T(8,128)(2,1)} %all-to-all-done), kind=kOutput, calls=%fused_computation.22 | convolution fusion | flops 226525184 | bytes 2785280 | tf_op jit(solution)/shard_map/dot_general | solution.py:64
  180.0 2.0 fusion.20
  182.0 1.4 copy.181
  183.4 5.7 %all-to-all-start.1 = ((bf16[16,8,18]{2,1,0:T(8,128)(2,1)}), bf16[16,8,18]{2,1,0:T(8,128)(2,1)}, u32[]{:S(2)}, u32[]{:S(2)}) async-start(bf16[16,8,18]{2,1,0:T(8,128)(2,1)} %bitcast.164), calls=%async_computation.1 | async-start | bytes 65536 | tf_op jit(solution)/shard_map/all_to_all | solution.py:175
  189.2 1.7 fusion.56
  190.9 45.8 %psum.14 = f32[19,256]{1,0:T(8,128)} all-reduce(f32[19,256]{1,0:T(8,128)} %fusion.56), channel_id=1, replica_groups=mesh['agent'=16,'dp_0'=16,'dp_1'=2] {'dp_0'}, use_global_device_ids=true, to_apply=%region_8.9 | all-reduce | flops 4864 | bytes 38912 | tf_op jit(solution)/shard_map/psum | solution.py:59
  236.7 17.5 %psum.15 = f32[19,256]{1,0:T(8,128)} all-reduce(f32[19,256]{1,0:T(8,128)} %psum.14), channel_id=1, replica_groups=mesh['agent'=16,'dp_0'=16,'dp_1'=2] {'dp_1'}, use_global_device_ids=true, to_apply=%region_9.10 | all-reduce | flops 4864 | bytes 38912 | tf_op jit(solution)/shard_map/psum | solution.py:59
  257.5 1.5 gather_fusion
  259.7 1.8 divide_subtract_fusion
  (96 shorter events, 62.0 us)
Async XLA Ops:
  7.2 69.9 %copy-start = (bf16[1,32,16,3456]{3,2,1,0:T(8,128)(2,1)S(1)}, bf16[1,32,16,3456]{3,2,1,0:T(8,128)(2,1)}, u32[]{:S(2)}) copy-start(bf16[1,32,16,3456]{3,2,1,0:T(8,128)(2,1)} %param.17) | copy-start | bytes 10616836
  7.2 63.8 %all-gather.4.cloned.1.call-start = ((), (), s32[]{:S(2)}) async-start(), calls=%async_computation.5 | async-start | bytes 2850816 | tf_op jit(solution)/shard_map/all_gather | solution.py:26
  46.0 129.6 %reduce-scatter.5.cloned.1.call-start = ((), (), s32[]{:S(2)}) async-start(), calls=%async_computation.4 | async-start | bytes 2850816 | tf_op jit(solution)/shard_map/reduce_scatter | solution.py:43
  46.8 37.5 %copy-start.7 = (s32[32,16]{1,0:T(8,128)}, s32[32,16]{1,0:T(8,128)S(1)}, u32[]{:S(2)}) copy-start(s32[32,16]{1,0:T(8,128)S(1)} %copy.182) | copy-start | bytes 6148
  71.0 3.0 %copy-start.12 = (bf16[1,32,3456]{2,1,0:T(8,128)(2,1)S(1)}, bf16[1,32,3456]{2,1,0:T(8,128)(2,1)}, u32[]{:S(2)}) copy-start(bf16[1,32,3456]{2,1,0:T(8,128)(2,1)} %param.18) | copy-start | bytes 663556
  72.7 1.3 copy-start.4
  77.1 6.1 %copy-start.8 = (bf16[1,19,256]{2,0,1:T(2,128)(2,1)S(1)}, bf16[1,19,256]{2,0,1:T(2,128)(2,1)}, u32[]{:S(2)}) copy-start(bf16[1,19,256]{2,0,1:T(2,128)(2,1)} %convert_element_type.81) | copy-start | bytes 29188
  79.7 0.8 copy-start.1
  82.5 0.7 copy-start.5
  143.7 3.3 %copy-start.2 = (f32[512,256]{1,0:T(8,128)S(1)}, f32[512,256]{1,0:T(8,128)}, u32[]{:S(2)}) copy-start(f32[512,256]{1,0:T(8,128)} %copy-done.1) | copy-start | bytes 1572868
  143.7 3.3 %copy-start.3 = (f32[512,256]{1,0:T(8,128)S(1)}, f32[512,256]{1,0:T(8,128)}, u32[]{:S(2)}) copy-start(f32[512,256]{1,0:T(8,128)} %get-tuple-element.223) | copy-start | bytes 1572868
  150.7 2.1 copy-start.6
  154.3 0.7 copy-start.11
  157.4 19.5 %all-to-all-start = ((bf16[16,8,3456]{2,1,0:T(8,128)(2,1)}), bf16[16,8,3456]{2,1,0:T(8,128)(2,1)}, u32[]{:S(2)}, u32[]{:S(2)}) async-start(bf16[16,8,3456]{2,1,0:T(8,128)(2,1)} %fusion.3), calls=%async_computation | async-start | bytes 1769472 | tf_op jit(solution)/shard_map/all_to_all | solution.py:169
  163.0 96.7 %reduce-scatter.7.cloned.1.call-start = ((), (), s32[]{:S(2)}) async-start(), calls=%async_computation.6 | async-start | bytes 1009664
  175.6 13.5 %copy-start.10 = (bf16[512,1]{0,1:T(2,128)(2,1)S(1)}, bf16[512,1]{0,1:T(2,128)(2,1)}, u32[]{:S(2)}) copy-start(bf16[512,1]{0,1:T(2,128)(2,1)} %concatenate.38) | copy-start | bytes 3076
  176.9 78.1 %copy-start.9 = (f32[32,19]{0,1:T(8,128)S(1)}, f32[32,19]{0,1:T(8,128)}, u32[]{:S(2)}) copy-start(f32[32,19]{0,1:T(8,128)} %fusion.26) | copy-start | bytes 7300
  183.4 74.1 %all-to-all-start.1 = ((bf16[16,8,18]{2,1,0:T(8,128)(2,1)}), bf16[16,8,18]{2,1,0:T(8,128)(2,1)}, u32[]{:S(2)}, u32[]{:S(2)}) async-start(bf16[16,8,18]{2,1,0:T(8,128)(2,1)} %bitcast.164), calls=%async_computation.1 | async-start | bytes 65536 | tf_op jit(solution)/shard_map/all_to_all | solution.py:175
Sparse Core Ops, SparseCore 0:
  46.1 24.8 all-gather.3
  154.5 21.0 reduce-scatter.4
  178.7 60.5 reduce-scatter.6
where the time goes:
time: 271 us; the launch traced here: 268 us
  blocking collectives  101 us (37%)
  local copies, waits for them, and re-layouts  46.2 us (17%)
  waiting for transfers between devices  35.5 us (13%)
  other arithmetic  35.2 us (13%)
  matrix products  24.1 us (9%)
  between operations  14.6 us (5%)
  starting transfers between devices  11.4 us (4%)
    psum x2, blocking collectives, by_axis(): x = lax.psum(x, axis)  63.3 us
    all_gather x1, blocking collectives, stacked_from(): blocks = lax.all_gather(blocks, axes[k], axis=0, tiled=True)  37.6 us
    all_gather x1, waiting for transfers between devices, stacked_from(): blocks = lax.all_gather(blocks, axes[k], axis=0, tiled=True)  22.9 us
    dynamic_update_slice x16, local copies, waits for them, and re-layouts, importance_trace_gradients(): lax.scan(backstep, start, (deltas.T, (discount * ratio).T), reverse=True)  20.6 us
    add x16, other arithmetic, backstep(): carry = delta + factor * carry  19.8 us
    dot_general x7, matrix products, contract(): lax.dot_general(left, right, (((1,), (1,)), ((), ())), preferred_element_...  13 us
    reduce_scatter x1, waiting for transfers between devices, reduced_to_own(): blocks = lax.psum_scatter(blocks, axes[k], scatter_dimension=0, tiled=True)  12.6 us
    unnamed x32, local copies, waits for them, and re-layouts  7.75 us
  transfers between devices with their start and end apart: 5, of which 2 were waited for; matrix products, arithmetic and copies ran while one was open for 7% of the time, Pallas kernels for 0%

commit v1 on v0

--- a/solution.py
+++ b/solution.py
@@ -12,6 +12,32 @@
 beta_first = 0.9
 beta_second = 0.99
 adam_eps = 1e-08
+
+
+def create_the_cards(q_in, d_out, target):
+    y_new, q_next = (q_in.shape[:d_out], q_in.shape[d_out + 1 :])
+    return jnp.moveaxis(q_in.reshape(*y_new, target, -1, *q_next), d_out, 0)
+
+
+def balance_frames(x0, axis_no):
+    u_next = list(x0.shape[1:])
+    u_next[axis_no] *= x0.shape[0]
+    return jnp.moveaxis(x0, 0, axis_no).reshape(u_next)
+
+
+def trace_screen_on_mesh(slab_in, mesh_dim, view, panel):
+    taken_in, later = (lax.axis_size(mesh_dim), lax.axis_index(mesh_dim))
+    mat_out = create_the_cards(slab_in, view, taken_in)
+    fields = [mat_out[later]]
+    j0 = 1
+    while j0 < taken_in:
+        tall = mat_out[(later + j0) % taken_in]
+        fields.append(
+            lax.ppermute(tall, mesh_dim, [(it, (it + j0) % taken_in) for it in range(taken_in)])
+        )
+        j0 = j0 + 1
+    mat_out = jnp.stack(fields, 0)[(later - jnp.arange(taken_in)) % taken_in]
+    return balance_frames(mat_out, panel)
 
 
 def joined_along(blocks, dim):
@@ -166,7 +192,7 @@
     ).astype(jnp.bfloat16)
     outgoing = jnp.dot(placing, opp_obs[0], preferred_element_type=jnp.float32).astype(jnp.bfloat16)
     outgoing = outgoing.reshape(agent_count, slots, width)
-    incoming = lax.all_to_all(outgoing, "agent", split_axis=0, concat_axis=0, tiled=True)
+    incoming = trace_screen_on_mesh(outgoing, "agent", 0, 0)
     count = incoming.shape[1]
     played = forward(incoming.reshape(agent_count * count, width), core_bf, head_bf)[0][
         :, :action_count

time: 271 us -> 323 us (1.19)
  starting transfers between devices: 11.4 us -> 60.7 us
  local copies, waits for them, and re-layouts: 46.2 us -> 68.8 us
  waiting for transfers between devices: 35.5 us -> 15.3 us
    ppermute x0 -> x15, starting transfers between devices: none -> 54.8 us  [trace_screen_on_mesh(): lax.ppermute(tall, mesh_dim, [(it, (it + j0) % taken_in) for it in range(...]
    all_gather x1, waiting for transfers between devices: 22.9 us -> 0.01 us  [stacked_from(): blocks = lax.all_gather(blocks, axes[k], axis=0, tiled=True)]
    unnamed x32 -> x46, local copies, waits for them, and re-layouts: 7.75 us -> 24 us
    all_to_all x1 -> x0, starting transfers between devices: 5.58 us -> none  [per_device(): lax.all_to_all(outgoing, 'agent', split_axis=0, concat_axis=0, tiled=True)]
  transfers between devices with their start and end apart: 5 -> 19, of which waited for: 2 -> 1; matrix products, arithmetic and copies ran while one was open for 7% -> 38% of each run, Pallas kernels for 0% -> 0%
where the time goes in v1:
time: 323 us; the launch traced here: 319 us
  blocking collectives  100 us (31%)
  local copies, waits for them, and re-layouts  68.8 us (21%)
  starting transfers between devices  60.7 us (19%)
  other arithmetic  35.6 us (11%)
  matrix products  24.1 us (7%)
  waiting for transfers between devices  15.3 us (5%)
  between operations  14.9 us (5%)
    psum x2, blocking collectives, by_axis(): x = lax.psum(x, axis)  62.4 us
    ppermute x15, starting transfers between devices, trace_screen_on_mesh(): lax.ppermute(tall, mesh_dim, [(it, (it + j0) % taken_in) for it in range(...  54.8 us
    all_gather x1, blocking collectives, stacked_from(): blocks = lax.all_gather(blocks, axes[k], axis=0, tiled=True)  37.6 us
    unnamed x46, local copies, waits for them, and re-layouts  24 us
    dynamic_update_slice x16, local copies, waits for them, and re-layouts, importance_trace_gradients(): lax.scan(backstep, start, (deltas.T, (discount * ratio).T), reverse=True)  20.6 us
    add x16, other arithmetic, backstep(): carry = delta + factor * carry  19.6 us
    reduce_scatter x1, waiting for transfers between devices, reduced_to_own(): blocks = lax.psum_scatter(blocks, axes[k], scatter_dimension=0, tiled=True)  15.2 us
    dot_general x7, matrix products, contract(): lax.dot_general(left, right, (((1,), (1,)), ((), ())), preferred_element_...  12.9 us
  transfers between devices with their start and end apart: 19, of which 1 were waited for; matrix products, arithmetic and copies ran while one was open for 38% of the time, Pallas kernels for 0%

profile of v1, /device:TPU:1, one launch (start us, length us, event | category | flops | bytes accessed | tf_op | source)
XLA Modules:
  0.0 319.4 jit_solution(1464454853503037495)
XLA Ops:
  8.3 37.6 %all-gather = bf16[16,8,3712]{2,1,0:T(8,128)(2,1)} all-gather(bf16[1,8,3712]{2,1,0:T(8,128)(2,1)S(1)} %convert_element_type.71), channel_id=2, replica_groups=mesh['agent'=16,'dp_0'=16,'dp_1'=2] {'dp_0'}, dimensions={0}, use_global_device_ids=true | all-gather | bytes 1009664 | tf_op jit(solution)/shard_map/all_gather | solution.py:52
  46.4 2.2 fusion.3
  48.6 2.1 dynamic-slice_bitcast_fusion
  50.7 3.2 %collective-permute-start = (bf16[1,8,3456]{2,1,0:T(8,128)(2,1)}, bf16[1,8,3456]{2,1,0:T(8,128)(2,1)}, u32[]{:S(2)}, u32[]{:S(2)}) collective-permute-start(bf16[1,8,3456]{2,1,0:T(8,128)(2,1)} %get-tuple-element.227), channel_id=1, source_target_pairs={{0,32},{32,64},{64,96},{96,128},{128,160},{160,192},{192,224},{224... | collective-permute-start | bytes 165896 | tf_op jit(solution)/shard_map/ppermute | solution.py:36
  53.9 4.5 %collective-permute-start.1 = (bf16[1,8,3456]{2,1,0:T(8,128)(2,1)}, bf16[1,8,3456]{2,1,0:T(8,128)(2,1)}, u32[]{:S(2)}, u32[]{:S(2)}) collective-permute-start(bf16[1,8,3456]{2,1,0:T(8,128)(2,1)} %get-tuple-element.226), channel_id=1, source_target_pairs={{0,64},{32,96},{64,128},{96,160},{128,192},{160,224},{192,256},{22... | collective-permute-start | bytes 165896 | tf_op jit(solution)/shard_map/ppermute | solution.py:36
  58.5 3.9 %collective-permute-start.2 = (bf16[1,8,3456]{2,1,0:T(8,128)(2,1)}, bf16[1,8,3456]{2,1,0:T(8,128)(2,1)}, u32[]{:S(2)}, u32[]{:S(2)}) collective-permute-start(bf16[1,8,3456]{2,1,0:T(8,128)(2,1)} %get-tuple-element.225), channel_id=1, source_target_pairs={{0,96},{32,128},{64,160},{96,192},{128,224},{160,256},{192,288},{2... | collective-permute-start | bytes 165896 | tf_op jit(solution)/shard_map/ppermute | solution.py:36
  62.4 3.1 collective-permute-start.3
  65.5 2.9 collective-permute-start.4
  72.5 3.1 collective-permute-start.5
  77.0 4.8 %collective-permute-start.6 = (bf16[1,8,3456]{2,1,0:T(8,128)(2,1)}, bf16[1,8,3456]{2,1,0:T(8,128)(2,1)S(1)}, u32[]{:S(2)}, u32[]{:S(2)}) collective-permute-start(bf16[1,8,3456]{2,1,0:T(8,128)(2,1)} %get-tuple-element.221), channel_id=1, source_target_pairs={{0,224},{32,256},{64,288},{96,320},{128,352},{160,384},{192,416},{... | collective-permute-start | bytes 165896 | tf_op jit(solution)/shard_map/ppermute | solution.py:36
  83.3 3.6 %collective-permute-start.7 = (bf16[1,8,3456]{2,1,0:T(8,128)(2,1)}, bf16[1,8,3456]{2,1,0:T(8,128)(2,1)S(1)}, u32[]{:S(2)}, u32[]{:S(2)}) collective-permute-start(bf16[1,8,3456]{2,1,0:T(8,128)(2,1)} %get-tuple-element.220), channel_id=1, source_target_pairs={{0,256},{32,288},{64,320},{96,352},{128,384},{160,416},{192,448},{... | collective-permute-start | bytes 165896 | tf_op jit(solution)/shard_map/ppermute | solution.py:36
  88.4 3.5 %collective-permute-start.8 = (bf16[1,8,3456]{2,1,0:T(8,128)(2,1)}, bf16[1,8,3456]{2,1,0:T(8,128)(2,1)S(1)}, u32[]{:S(2)}, u32[]{:S(2)}) collective-permute-start(bf16[1,8,3456]{2,1,0:T(8,128)(2,1)} %get-tuple-element.219), channel_id=1, source_target_pairs={{0,288},{32,320},{64,352},{96,384},{128,416},{160,448},{192,480},{... | collective-permute-start | bytes 165896 | tf_op jit(solution)/shard_map/ppermute | solution.py:36
  93.4 5.3 %collective-permute-start.9 = (bf16[1,8,3456]{2,1,0:T(8,128)(2,1)}, bf16[1,8,3456]{2,1,0:T(8,128)(2,1)}, u32[]{:S(2)}, u32[]{:S(2)}) collective-permute-start(bf16[1,8,3456]{2,1,0:T(8,128)(2,1)} %get-tuple-element.218), channel_id=1, source_target_pairs={{0,320},{32,352},{64,384},{96,416},{128,448},{160,480},{192,0},{22... | collective-permute-start | bytes 165896 | tf_op jit(solution)/shard_map/ppermute | solution.py:36
  100.2 4.8 %collective-permute-start.10 = (bf16[1,8,3456]{2,1,0:T(8,128)(2,1)}, bf16[1,8,3456]{2,1,0:T(8,128)(2,1)}, u32[]{:S(2)}, u32[]{:S(2)}) collective-permute-start(bf16[1,8,3456]{2,1,0:T(8,128)(2,1)} %get-tuple-element.217), channel_id=1, source_target_pairs={{0,352},{32,384},{64,416},{96,448},{128,480},{160,0},{192,32},{224... | collective-permute-start | bytes 165896 | tf_op jit(solution)/shard_map/ppermute | solution.py:36
  105.6 3.8 %collective-permute-start.11 = (bf16[1,8,3456]{2,1,0:T(8,128)(2,1)}, bf16[1,8,3456]{2,1,0:T(8,128)(2,1)}, u32[]{:S(2)}, u32[]{:S(2)}) collective-permute-start(bf16[1,8,3456]{2,1,0:T(8,128)(2,1)} %get-tuple-element.216), channel_id=1, source_target_pairs={{0,384},{32,416},{64,448},{96,480},{128,0},{160,32},{192,64},{224,... | collective-permute-start | bytes 165896 | tf_op jit(solution)/shard_map/ppermute | solution.py:36
  110.0 1.9 collective-permute-start.12
  112.5 2.5 collective-permute-start.13
  121.7 2.6 fusion.4
  125.1 2.0 add_convert_fusion
  128.9 2.3 fusion.33
  136.3 40.2 %while.17 = (s32[]{:T(128)}, f32[32]{0:T(128)}, f32[16,32]{1,0:T(8,128)}, f32[16,32]{1,0:T(8,128)}, f32[16,32]{1,0:T(8,128)}, /*index=5*/s32[]{:T(128)}, s32[]{:T(128)}, s32[]{:T(128)}) while((s32[]{:T(128)}, f32[32]{0:T(128)}, f32[16,32]{1,0:T(8,128)}, f32[16,32]{1,0:T(8,128)}, f32[16,32]{1,0:T(8,128)}, /*index=5*/s32[]{:T(128)}, ...), condition=%wide.region_4.5_spmd.clone, body=%wide.region_3.4_spmd.clone.sunk | while | flops 100 | bytes 891 | solution.py:135
  184.6 1.9 fusion.31
  189.2 2.1 convolution_convert_fusion.2
  195.0 2.1 convolution_convert_fusion
  198.7 3.7 %collective-permute-start.14 = (bf16[1,8,3456]{2,1,0:T(8,128)(2,1)}, bf16[1,8,3456]{2,1,0:T(8,128)(2,1)}, u32[]{:S(2)}, u32[]{:S(2)}) collective-permute-start(bf16[1,8,3456]{2,1,0:T(8,128)(2,1)} %get-tuple-element.213), channel_id=1, source_target_pairs={{0,480},{32,0},{64,32},{96,64},{128,96},{160,128},{192,160},{224,1... | collective-permute-start | bytes 165896 | tf_op jit(solution)/shard_map/ppermute | solution.py:36
  209.7 15.2 %reduce-scatter.5.cloned.1.call-done = bf16[16,8,3712]{2,1,0:T(8,128)(2,1)} async-done(((bf16[32,8,3712]{2,1,0:T(8,128)(2,1)}), bf16[16,8,3712]{2,1,0:T(8,128)(2,1)}) %reduce-scatter.5.cloned.1.call-update) | async-done | bytes 950288 | tf_op jit(solution)/shard_map/reduce_scatter | solution.py:69
  226.3 2.9 gather_fusion
  229.2 3.1 fusion.15
  232.3 2.0 fusion.20
  235.7 5.7 %all-to-all-start = ((bf16[16,8,18]{2,1,0:T(8,128)(2,1)}), bf16[16,8,18]{2,1,0:T(8,128)(2,1)}, u32[]{:S(2)}, u32[]{:S(2)}) async-start(bf16[16,8,18]{2,1,0:T(8,128)(2,1)} %bitcast.228), calls=%async_computation | async-start | bytes 65536 | tf_op jit(solution)/shard_map/all_to_all | solution.py:201
  243.2 45.4 %psum.14 = f32[19,256]{1,0:T(8,128)} all-reduce(f32[19,256]{1,0:T(8,128)} %fusion.56), channel_id=1, replica_groups=mesh['agent'=16,'dp_0'=16,'dp_1'=2] {'dp_0'}, use_global_device_ids=true, to_apply=%region_8.9 | all-reduce | flops 4864 | bytes 38912 | tf_op jit(solution)/shard_map/psum | solution.py:85
  288.5 17.0 %psum.15 = f32[19,256]{1,0:T(8,128)} all-reduce(f32[19,256]{1,0:T(8,128)} %psum.14), channel_id=1, replica_groups=mesh['agent'=16,'dp_0'=16,'dp_1'=2] {'dp_1'}, use_global_device_ids=true, to_apply=%region_9.10 | all-reduce | flops 4864 | bytes 38912 | tf_op jit(solution)/shard_map/psum | solution.py:85
  (143 shorter events, 103.4 us)
Async XLA Ops:
  7.2 114.5 %copy-start = (bf16[1,32,16,3456]{3,2,1,0:T(8,128)(2,1)S(1)}, bf16[1,32,16,3456]{3,2,1,0:T(8,128)(2,1)}, u32[]{:S(2)}) copy-start(bf16[1,32,16,3456]{3,2,1,0:T(8,128)(2,1)} %param.17) | copy-start | bytes 10616836
  7.2 39.0 %copy-start.11 = (s32[1,32,1]{1,2,0:T(1,128)S(1)}, s32[1,32,1]{1,2,0:T(1,128)}, u32[]{:S(2)}) copy-start(s32[1,32,1]{1,2,0:T(1,128)} %param.20) | copy-start | bytes 388
  7.2 108.5 %all-gather.4.cloned.1.call-start = ((), (), s32[]{:S(2)}) async-start(), calls=%async_computation.4 | async-start | bytes 2850816 | tf_op jit(solution)/shard_map/all_gather | solution.py:52
  46.0 178.9 %reduce-scatter.5.cloned.1.call-start = ((), (), s32[]{:S(2)}) async-start(), calls=%async_computation.3 | async-start | bytes 2850816 | tf_op jit(solution)/shard_map/reduce_scatter | solution.py:69
  50.7 21.8 %collective-permute-start = (bf16[1,8,3456]{2,1,0:T(8,128)(2,1)}, bf16[1,8,3456]{2,1,0:T(8,128)(2,1)}, u32[]{:S(2)}, u32[]{:S(2)}) collective-permute-start(bf16[1,8,3456]{2,1,0:T(8,128)(2,1)} %get-tuple-element.227), channel_id=1, source_target_pairs={{0,32},{32,64},{64,96},{96,128},{128,160},{160,192},{192,224},{224... | collective-permute-start | bytes 165896 | tf_op jit(solution)/shard_map/ppermute | solution.py:36
  53.9 23.1 %collective-permute-start.1 = (bf16[1,8,3456]{2,1,0:T(8,128)(2,1)}, bf16[1,8,3456]{2,1,0:T(8,128)(2,1)}, u32[]{:S(2)}, u32[]{:S(2)}) collective-permute-start(bf16[1,8,3456]{2,1,0:T(8,128)(2,1)} %get-tuple-element.226), channel_id=1, source_target_pairs={{0,64},{32,96},{64,128},{96,160},{128,192},{160,224},{192,256},{22... | collective-permute-start | bytes 165896 | tf_op jit(solution)/shard_map/ppermute | solution.py:36
  58.5 24.8 %collective-permute-start.2 = (bf16[1,8,3456]{2,1,0:T(8,128)(2,1)}, bf16[1,8,3456]{2,1,0:T(8,128)(2,1)}, u32[]{:S(2)}, u32[]{:S(2)}) collective-permute-start(bf16[1,8,3456]{2,1,0:T(8,128)(2,1)} %get-tuple-element.225), channel_id=1, source_target_pairs={{0,96},{32,128},{64,160},{96,192},{128,224},{160,256},{192,288},{2... | collective-permute-start | bytes 165896 | tf_op jit(solution)/shard_map/ppermute | solution.py:36
  62.4 26.0 %collective-permute-start.3 = (bf16[1,8,3456]{2,1,0:T(8,128)(2,1)}, bf16[1,8,3456]{2,1,0:T(8,128)(2,1)}, u32[]{:S(2)}, u32[]{:S(2)}) collective-permute-start(bf16[1,8,3456]{2,1,0:T(8,128)(2,1)} %get-tuple-element.224), channel_id=1, source_target_pairs={{0,128},{32,160},{64,192},{96,224},{128,256},{160,288},{192,320},{... | collective-permute-start | bytes 165896 | tf_op jit(solution)/shard_map/ppermute | solution.py:36
  65.5 27.9 %collective-permute-start.4 = (bf16[1,8,3456]{2,1,0:T(8,128)(2,1)}, bf16[1,8,3456]{2,1,0:T(8,128)(2,1)}, u32[]{:S(2)}, u32[]{:S(2)}) collective-permute-start(bf16[1,8,3456]{2,1,0:T(8,128)(2,1)} %get-tuple-element.223), channel_id=1, source_target_pairs={{0,160},{32,192},{64,224},{96,256},{128,288},{160,320},{192,352},{... | collective-permute-start | bytes 165896 | tf_op jit(solution)/shard_map/ppermute | solution.py:36
  71.1 57.8 %copy-start.7 = (s32[32,16]{1,0:T(8,128)}, s32[32,16]{1,0:T(8,128)S(1)}, u32[]{:S(2)}) copy-start(s32[32,16]{1,0:T(8,128)S(1)} %copy.182) | copy-start | bytes 6148
  72.5 27.7 %collective-permute-start.5 = (bf16[1,8,3456]{2,1,0:T(8,128)(2,1)}, bf16[1,8,3456]{2,1,0:T(8,128)(2,1)S(1)}, u32[]{:S(2)}, u32[]{:S(2)}) collective-permute-start(bf16[1,8,3456]{2,1,0:T(8,128)(2,1)} %get-tuple-element.222), channel_id=1, source_target_pairs={{0,192},{32,224},{64,256},{96,288},{128,320},{160,352},{192,384},{... | collective-permute-start | bytes 165896 | tf_op jit(solution)/shard_map/ppermute | solution.py:36
  77.0 28.5 %collective-permute-start.6 = (bf16[1,8,3456]{2,1,0:T(8,128)(2,1)}, bf16[1,8,3456]{2,1,0:T(8,128)(2,1)S(1)}, u32[]{:S(2)}, u32[]{:S(2)}) collective-permute-start(bf16[1,8,3456]{2,1,0:T(8,128)(2,1)} %get-tuple-element.221), channel_id=1, source_target_pairs={{0,224},{32,256},{64,288},{96,320},{128,352},{160,384},{192,416},{... | collective-permute-start | bytes 165896 | tf_op jit(solution)/shard_map/ppermute | solution.py:36
  83.3 26.7 %collective-permute-start.7 = (bf16[1,8,3456]{2,1,0:T(8,128)(2,1)}, bf16[1,8,3456]{2,1,0:T(8,128)(2,1)S(1)}, u32[]{:S(2)}, u32[]{:S(2)}) collective-permute-start(bf16[1,8,3456]{2,1,0:T(8,128)(2,1)} %get-tuple-element.220), channel_id=1, source_target_pairs={{0,256},{32,288},{64,320},{96,352},{128,384},{160,416},{192,448},{... | collective-permute-start | bytes 165896 | tf_op jit(solution)/shard_map/ppermute | solution.py:36
  88.4 24.2 %collective-permute-start.8 = (bf16[1,8,3456]{2,1,0:T(8,128)(2,1)}, bf16[1,8,3456]{2,1,0:T(8,128)(2,1)S(1)}, u32[]{:S(2)}, u32[]{:S(2)}) collective-permute-start(bf16[1,8,3456]{2,1,0:T(8,128)(2,1)} %get-tuple-element.219), channel_id=1, source_target_pairs={{0,288},{32,320},{64,352},{96,384},{128,416},{160,448},{192,480},{... | collective-permute-start | bytes 165896 | tf_op jit(solution)/shard_map/ppermute | solution.py:36
  93.4 105.3 %collective-permute-start.9 = (bf16[1,8,3456]{2,1,0:T(8,128)(2,1)}, bf16[1,8,3456]{2,1,0:T(8,128)(2,1)}, u32[]{:S(2)}, u32[]{:S(2)}) collective-permute-start(bf16[1,8,3456]{2,1,0:T(8,128)(2,1)} %get-tuple-element.218), channel_id=1, source_target_pairs={{0,320},{32,352},{64,384},{96,416},{128,448},{160,480},{192,0},{22... | collective-permute-start | bytes 165896 | tf_op jit(solution)/shard_map/ppermute | solution.py:36
  100.2 103.8 %collective-permute-start.10 = (bf16[1,8,3456]{2,1,0:T(8,128)(2,1)}, bf16[1,8,3456]{2,1,0:T(8,128)(2,1)}, u32[]{:S(2)}, u32[]{:S(2)}) collective-permute-start(bf16[1,8,3456]{2,1,0:T(8,128)(2,1)} %get-tuple-element.217), channel_id=1, source_target_pairs={{0,352},{32,384},{64,416},{96,448},{128,480},{160,0},{192,32},{224... | collective-permute-start | bytes 165896 | tf_op jit(solution)/shard_map/ppermute | solution.py:36
  105.6 99.8 %collective-permute-start.11 = (bf16[1,8,3456]{2,1,0:T(8,128)(2,1)}, bf16[1,8,3456]{2,1,0:T(8,128)(2,1)}, u32[]{:S(2)}, u32[]{:S(2)}) collective-permute-start(bf16[1,8,3456]{2,1,0:T(8,128)(2,1)} %get-tuple-element.216), channel_id=1, source_target_pairs={{0,384},{32,416},{64,448},{96,480},{128,0},{160,32},{192,64},{224,... | collective-permute-start | bytes 165896 | tf_op jit(solution)/shard_map/ppermute | solution.py:36
  110.0 96.8 %collective-permute-start.12 = (bf16[1,8,3456]{2,1,0:T(8,128)(2,1)}, bf16[1,8,3456]{2,1,0:T(8,128)(2,1)}, u32[]{:S(2)}, u32[]{:S(2)}) collective-permute-start(bf16[1,8,3456]{2,1,0:T(8,128)(2,1)} %get-tuple-element.215), channel_id=1, source_target_pairs={{0,416},{32,448},{64,480},{96,0},{128,32},{160,64},{192,96},{224,1... | collective-permute-start | bytes 165896 | tf_op jit(solution)/shard_map/ppermute | solution.py:36
  112.5 95.7 %collective-permute-start.13 = (bf16[1,8,3456]{2,1,0:T(8,128)(2,1)}, bf16[1,8,3456]{2,1,0:T(8,128)(2,1)}, u32[]{:S(2)}, u32[]{:S(2)}) collective-permute-start(bf16[1,8,3456]{2,1,0:T(8,128)(2,1)} %get-tuple-element.214), channel_id=1, source_target_pairs={{0,448},{32,480},{64,0},{96,32},{128,64},{160,96},{192,128},{224,1... | collective-permute-start | bytes 165896 | tf_op jit(solution)/shard_map/ppermute | solution.py:36
  115.7 3.0 copy-start.12
  117.4 1.3 copy-start.4
  121.7 6.1 %copy-start.8 = (bf16[1,19,256]{2,0,1:T(2,128)(2,1)S(1)}, bf16[1,19,256]{2,0,1:T(2,128)(2,1)}, u32[]{:S(2)}) copy-start(bf16[1,19,256]{2,0,1:T(2,128)(2,1)} %convert_element_type.81) | copy-start | bytes 29188
  124.3 0.8 copy-start.1
  127.1 0.7 copy-start.5
  188.1 3.2 %copy-start.2 = (f32[512,256]{1,0:T(8,128)S(1)}, f32[512,256]{1,0:T(8,128)}, u32[]{:S(2)}) copy-start(f32[512,256]{1,0:T(8,128)} %copy-done.1) | copy-start | bytes 1572868
  188.1 3.2 %copy-start.3 = (f32[512,256]{1,0:T(8,128)S(1)}, f32[512,256]{1,0:T(8,128)}, u32[]{:S(2)}) copy-start(f32[512,256]{1,0:T(8,128)} %get-tuple-element.239) | copy-start | bytes 1572868
  195.0 2.1 copy-start.6
  198.7 112.4 %reduce-scatter.7.cloned.1.call-start = ((), (), s32[]{:S(2)}) async-start(), calls=%async_computation.5 | async-start | bytes 1009664
  198.7 26.1 %collective-permute-start.14 = (bf16[1,8,3456]{2,1,0:T(8,128)(2,1)}, bf16[1,8,3456]{2,1,0:T(8,128)(2,1)}, u32[]{:S(2)}, u32[]{:S(2)}) collective-permute-start(bf16[1,8,3456]{2,1,0:T(8,128)(2,1)} %get-tuple-element.213), channel_id=1, source_target_pairs={{0,480},{32,0},{64,32},{96,64},{128,96},{160,128},{192,160},{224,1... | collective-permute-start | bytes 165896 | tf_op jit(solution)/shard_map/ppermute | solution.py:36
  229.2 12.2 %copy-start.10 = (bf16[512,1]{0,1:T(2,128)(2,1)S(1)}, bf16[512,1]{0,1:T(2,128)(2,1)}, u32[]{:S(2)}) copy-start(bf16[512,1]{0,1:T(2,128)(2,1)} %concatenate.38) | copy-start | bytes 3076
  229.2 77.2 %copy-start.9 = (f32[32,19]{0,1:T(8,128)S(1)}, f32[32,19]{0,1:T(8,128)}, u32[]{:S(2)}) copy-start(f32[32,19]{0,1:T(8,128)} %fusion.26) | copy-start | bytes 7300
  235.7 73.2 %all-to-all-start = ((bf16[16,8,18]{2,1,0:T(8,128)(2,1)}), bf16[16,8,18]{2,1,0:T(8,128)(2,1)}, u32[]{:S(2)}, u32[]{:S(2)}) async-start(bf16[16,8,18]{2,1,0:T(8,128)(2,1)} %bitcast.228), calls=%async_computation | async-start | bytes 65536 | tf_op jit(solution)/shard_map/all_to_all | solution.py:201
Sparse Core Ops, SparseCore 0:
  46.1 24.8 all-gather.3
  198.8 26.0 reduce-scatter.4
  227.9 61.1 reduce-scatter.6
